TPU v7x, 512 devices: a whole 4x4x16 slice. The times are simulated.
512 devices in a mesh: src: 16 (over z), tgt: 32 (over x, y, core).
Axes of the slice: x: 4, y: 4, z: 16, core: 2. Of those that a mesh axis runs over, the one named last changes fastest.
Arguments:
- src_points: bfloat16 [16, 8192, 256], P('src', 'tgt'), may hold values from -4 to 4
- src_logmass: bfloat16 [16, 8192], P('src', 'tgt'), may hold values from -1 to 1
- tgt_points: bfloat16 [32, 4096, 256], P('tgt', 'src'), may hold values from -4 to 4
- tgt_logmass: bfloat16 [32, 4096], P('tgt', 'src'), may hold values from -1 to 1
- tile_list: int32 [16, 32, 80, 2], P('src', 'tgt'), may hold values from 0 to 63, as said below
- tile_count: int32 [16, 32], P('src', 'tgt'), may hold values from 64 to 80, as said below
Outputs:
- src_potential: float32 [16, 8192], P('src', 'tgt')
- tgt_potential: float32 [32, 4096], P('tgt', 'src')
Inputs may be any that keep to these rules, and one draw needn't show every extreme that they name: `tile_list`: live slots hold distinct pairs (row tile, column tile) with row tile below 64 and column tile below 32; slot r < 64 holds (r, r mod 32); slots at or beyond the count hold (0, 0). `tile_count`: at most 80; exactly 80 for some block pair in every draw.
All inputs are finite; a program needn't handle non-finite values.
Results may differ from a plain program's by a relative error of at most 0.02.
Values may be sent and summed in bfloat16 or wider, within the bound.
A program may use at most 64 MiB of HBM per device.

v0:
```python
import jax
import jax.numpy as jnp
from jax import lax
from jax.sharding import PartitionSpec as P

TILE = 128
ITERS = 3


inverse_eps = 20.0
lowest_log = -1e30
slot_group = 8


def tile_block(sources, targets, row_ids, col_ids):
    left_rows = jnp.take(sources, row_ids, axis=0)
    right_rows = jnp.take(targets, col_ids, axis=0)
    products = jnp.einsum("sad,sbd->sab", left_rows, right_rows, preferred_element_type=jnp.float32)
    return (1.0 - products).astype(jnp.bfloat16)


def fold_into(carried, owners, tile_peak, tile_total):
    peaks, totals = carried
    candidate = jnp.where(owners[:, :, None], tile_peak[:, None, :], lowest_log).max(axis=0)
    highest = jnp.maximum(peaks, candidate)
    shortfall = jnp.minimum(tile_peak[:, None, :] - highest[None, :, :], 0.0)
    added = jnp.where(owners[:, :, None], tile_total[:, None, :] * jnp.exp(shortfall), 0.0).sum(
        axis=0
    )
    return (highest, totals * jnp.exp(peaks - highest) + added)


def settle_rows(peaks, totals, log_mass):
    highest = lax.pmax(peaks.astype(jnp.bfloat16), "tgt").astype(peaks.dtype)
    summed = lax.psum((totals * jnp.exp(peaks - highest)).astype(jnp.bfloat16), "tgt").astype(
        jnp.float32
    )
    return log_mass - (highest + jnp.log(summed))


def settle_cols(peaks, totals, log_mass):
    highest = lax.pmax(peaks, "src")
    summed = lax.psum(totals * jnp.exp(peaks - highest), "src")
    return log_mass - (highest + jnp.log(summed))


def shards(src_points, src_logmass, tgt_points, tgt_logmass, tile_list, tile_count):
    sources, mass_a = (
        lax.all_gather(src_points, "tgt", axis=1, tiled=True),
        lax.all_gather(src_logmass, "tgt", axis=1, tiled=True),
    )
    targets, mass_b = (
        lax.all_gather(tgt_points, "src", axis=1, tiled=True),
        lax.all_gather(tgt_logmass, "src", axis=1, tiled=True),
    )
    features = sources.shape[2]
    row_tiles = sources.shape[1] // TILE
    col_tiles = targets.shape[1] // TILE
    sources = sources.reshape(row_tiles, TILE, features)
    targets = targets.reshape(col_tiles, TILE, features)
    log_mass_a = mass_a.reshape(row_tiles, TILE).astype(jnp.float32)
    log_mass_b = mass_b.reshape(col_tiles, TILE).astype(jnp.float32)
    row_ids = tile_list[0, 0, :, 0]
    col_ids = tile_list[0, 0, :, 1]
    live_count = tile_count[0, 0]
    group_count = (live_count + slot_group - 1) // slot_group
    row_range = jnp.arange(row_tiles, dtype=jnp.int32)
    col_range = jnp.arange(col_tiles, dtype=jnp.int32)

    def group_tiles(group):
        first_slot = group * slot_group
        tile_rows = lax.dynamic_slice_in_dim(row_ids, first_slot, slot_group)
        tile_cols = lax.dynamic_slice_in_dim(col_ids, first_slot, slot_group)
        live_slots = first_slot + jnp.arange(slot_group, dtype=jnp.int32) < live_count
        tile_cost = tile_block(sources, targets, tile_rows, tile_cols)
        return (tile_cost, tile_rows, tile_cols, live_slots)

    column_pot = jnp.zeros((col_tiles, TILE), jnp.float32)
    row_pot = jnp.zeros((row_tiles, TILE), jnp.float32)
    for sweep in range(ITERS):

        def row_advance(group, carried):
            tile_cost, tile_rows, tile_cols, live_slots = group_tiles(group)
            scores = jnp.take(column_pot, tile_cols, axis=0)[
                :, None, :
            ] - inverse_eps * tile_cost.astype(jnp.float32)
            tile_peak = scores.max(axis=2)
            tile_total = jnp.exp(scores - tile_peak[:, :, None]).sum(axis=2)
            owners = (tile_rows[:, None] == row_range[None, :]) & live_slots[:, None]
            return fold_into(carried, owners, tile_peak, tile_total)

        row_initial = (
            jnp.full((row_tiles, TILE), lowest_log, jnp.float32),
            jnp.zeros((row_tiles, TILE), jnp.float32),
        )
        peaks, totals = lax.fori_loop(0, group_count, row_advance, row_initial)
        row_pot = settle_rows(peaks, totals, log_mass_a)

        def col_advance(group, carried):
            tile_cost, tile_rows, tile_cols, live_slots = group_tiles(group)
            scores = jnp.take(row_pot, tile_rows, axis=0)[
                :, :, None
            ] - inverse_eps * tile_cost.astype(jnp.float32)
            tile_peak = scores.max(axis=1)
            tile_total = jnp.exp(scores - tile_peak[:, None, :]).sum(axis=1)
            owners = (tile_cols[:, None] == col_range[None, :]) & live_slots[:, None]
            return fold_into(carried, owners, tile_peak, tile_total)

        initial = (
            jnp.full((col_tiles, TILE), lowest_log, jnp.float32),
            jnp.zeros((col_tiles, TILE), jnp.float32),
        )
        peaks, totals = lax.fori_loop(0, group_count, col_advance, initial)
        column_pot = settle_cols(peaks, totals, log_mass_b)
    own_rows = src_points.shape[1]
    own_cols = tgt_points.shape[1]
    src_out = lax.dynamic_slice_in_dim(
        row_pot.reshape(-1), lax.axis_index("tgt") * own_rows, own_rows
    )
    tgt_out = lax.dynamic_slice_in_dim(
        column_pot.reshape(-1), lax.axis_index("src") * own_cols, own_cols
    )
    return (src_out.reshape(1, own_rows), tgt_out.reshape(1, own_cols))


def solution(mesh):
    placed = (
        P("src", "tgt", None),
        P("src", "tgt"),
        P("tgt", "src", None),
        P("tgt", "src"),
        P("src", "tgt", None, None),
        P("src", "tgt"),
    )
    return jax.shard_map(
        shards,
        mesh=mesh,
        in_specs=placed,
        out_specs=(P("src", "tgt"), P("tgt", "src")),
        check_vma=False,
    )
```

profile of v0, /device:TPU:32, one launch (start us, length us, event | category | flops | bytes accessed | tf_op | source)
XLA Modules:
  0.0 1656.8 jit_solution(466419633274846200)
XLA Ops:
  9.3 24.5 %all_gather.12 = bf16[1,8192]{1,0:T(2,128)(2,1)S(1)} all-gather(bf16[1,256]{1,0:T(2,128)(2,1)} %param.27), channel_id=1, replica_groups=mesh['src'=16,'tgt'=32] {'tgt'}, dimensions={1}, use_global_device_ids=true | all-gather | bytes 16896 | tf_op jit(solution)/shard_map/all_gather | solution.py:50
  33.8 33.5 %all_gather.13 = bf16[1,4096]{1,0:T(2,128)(2,1)S(1)} all-gather(bf16[1,256]{1,0:T(2,128)(2,1)} %param.29), channel_id=1, replica_groups=mesh['src'=16,'tgt'=32] {'src'}, dimensions={1}, use_global_device_ids=true | all-gather | bytes 8704 | tf_op jit(solution)/shard_map/all_gather | solution.py:54
  68.1 19.2 %all-gather.5.cloned.1.call-done = bf16[1,4096,256]{2,1,0:T(8,128)(2,1)} async-done(((bf16[1,256,256]{2,1,0:T(8,128)(2,1)}), bf16[1,4096,256]{2,1,0:T(8,128)(2,1)}) %all-gather.5.cloned.1.call-update) | async-done | bytes 2097168 | tf_op jit(solution)/shard_map/all_gather | solution.py:53
  87.3 61.4 %all-gather.3.cloned.1.call-done = bf16[1,8192,256]{2,1,0:T(8,128)(2,1)} async-done(((bf16[1,256,256]{2,1,0:T(8,128)(2,1)}), bf16[1,8192,256]{2,1,0:T(8,128)(2,1)}) %all-gather.3.cloned.1.call-update) | async-done | bytes 4194320 | tf_op jit(solution)/shard_map/all_gather | solution.py:49
  148.8 65.7 %while.78 = (s32[]{:T(128)}, f32[64,128]{1,0:T(8,128)S(1)}, f32[64,128]{1,0:T(8,128)S(1)}, s32[]{:T(128)}, s32[80]{0:T(128)S(1)}, /*index=5*/s32[]{:T(128)}, s32...) while((s32[]{:T(128)}, f32[64,128]{1,0:T(8,128)S(1)}, ...), condition=%wide.region_5.9_spmd.clone, body=%wide.region_0.8_spmd.clone.sunk | while | flops 69159056 | bytes 4692091 | solution.py:96
  214.5 126.3 %pmax.42 = bf16[64,128]{1,0:T(8,128)(2,1)S(1)} all-reduce(bf16[64,128]{1,0:T(8,128)(2,1)S(1)} %convert_element_type.88), channel_id=1, replica_groups=mesh['src'=16,'tgt'=32] {'tgt'}, use_global_device_ids=true, to_apply=%region_6.10 | all-reduce | flops 8192 | bytes 32768 | tf_op jit(solution)/shard_map/pmax | solution.py:34
  340.8 123.8 %psum.42 = bf16[64,128]{1,0:T(8,128)(2,1)S(1)} all-reduce(bf16[64,128]{1,0:T(8,128)(2,1)S(1)} %fusion.80), channel_id=1, replica_groups=mesh['src'=16,'tgt'=32] {'tgt'}, use_global_device_ids=true, to_apply=%region_7.11 | all-reduce | flops 8192 | bytes 32768 | tf_op jit(solution)/shard_map/psum | solution.py:35
  464.7 64.9 %while.79 = (s32[]{:T(128)}, f32[32,128]{1,0:T(8,128)S(1)}, f32[32,128]{1,0:T(8,128)S(1)}, s32[]{:T(128)}, s32[80]{0:T(128)S(1)}, /*index=5*/s32[]{:T(128)}, s32...) while((s32[]{:T(128)}, f32[32,128]{1,0:T(8,128)S(1)}, ...), condition=%wide.region_13.18_spmd.clone, body=%wide.region_8.0_spmd.clone.sunk | while | flops 68920976 | bytes 4461943 | solution.py:113
  467.6 2.8 gather_fusion.4
  474.8 2.8 gather_fusion.4
  482.1 2.8 gather_fusion.4
  489.3 2.8 gather_fusion.4
  496.5 2.8 gather_fusion.4
  503.7 2.8 gather_fusion.4
  510.9 2.8 gather_fusion.4
  518.1 2.8 gather_fusion.4
  525.3 2.8 gather_fusion.4
  529.6 65.7 %pmax.43 = f32[32,128]{1,0:T(8,128)S(1)} all-reduce(f32[32,128]{1,0:T(8,128)S(1)} %get-tuple-element.357), channel_id=1, replica_groups=mesh['src'=16,'tgt'=32] {'src'}, use_global_device_ids=true, to_apply=%region_14.19 | all-reduce | flops 4096 | bytes 32768 | tf_op jit(solution)/shard_map/pmax | solution.py:42
  595.4 55.7 %psum.43 = f32[32,128]{1,0:T(8,128)S(1)} all-reduce(f32[32,128]{1,0:T(8,128)S(1)} %exponential_multiply_fusion.2), channel_id=1, replica_groups=mesh['src'=16,'tgt'=32] {'src'}, use_global_device_ids=true, to_apply=%region_15.20 | all-reduce | flops 4096 | bytes 32768 | tf_op jit(solution)/shard_map/psum | solution.py:43
  651.1 65.6 %while.80 = (s32[]{:T(128)}, f32[64,128]{1,0:T(8,128)S(1)}, f32[64,128]{1,0:T(8,128)S(1)}, s32[]{:T(128)}, s32[80]{0:T(128)S(1)}, /*index=5*/s32[]{:T(128)}, s32...) while((s32[]{:T(128)}, f32[64,128]{1,0:T(8,128)S(1)}, ...), condition=%wide.region_21.26_spmd.clone, body=%wide.region_16.25_spmd.clone.sunk | while | flops 69159056 | bytes 4675703 | solution.py:96
  716.7 123.8 %pmax.44 = bf16[64,128]{1,0:T(8,128)(2,1)S(1)} all-reduce(bf16[64,128]{1,0:T(8,128)(2,1)S(1)} %convert_element_type.92), channel_id=1, replica_groups=mesh['src'=16,'tgt'=32] {'tgt'}, use_global_device_ids=true, to_apply=%region_22.27 | all-reduce | flops 8192 | bytes 32768 | tf_op jit(solution)/shard_map/pmax | solution.py:34
  840.6 123.8 %psum.44 = bf16[64,128]{1,0:T(8,128)(2,1)S(1)} all-reduce(bf16[64,128]{1,0:T(8,128)(2,1)S(1)} %fusion.84), channel_id=1, replica_groups=mesh['src'=16,'tgt'=32] {'tgt'}, use_global_device_ids=true, to_apply=%region_23.28 | all-reduce | flops 8192 | bytes 32768 | tf_op jit(solution)/shard_map/psum | solution.py:35
  964.5 64.9 %while.81 = (s32[]{:T(128)}, f32[32,128]{1,0:T(8,128)S(1)}, f32[32,128]{1,0:T(8,128)S(1)}, s32[]{:T(128)}, s32[80]{0:T(128)S(1)}, /*index=5*/s32[]{:T(128)}, s32...) while((s32[]{:T(128)}, f32[32,128]{1,0:T(8,128)S(1)}, ...), condition=%wide.region_29.34_spmd.clone, body=%wide.region_24.33_spmd.clone.sunk | while | flops 68920976 | bytes 4461943 | solution.py:113
  967.4 2.8 gather_fusion.10
  974.6 2.8 gather_fusion.10
  981.8 2.8 gather_fusion.10
  989.1 2.8 gather_fusion.10
  996.3 2.8 gather_fusion.10
  1003.5 2.8 gather_fusion.10
  1010.7 2.8 gather_fusion.10
  1017.9 2.8 gather_fusion.10
  1025.1 2.8 gather_fusion.10
  1029.4 64.8 %pmax.45 = f32[32,128]{1,0:T(8,128)S(1)} all-reduce(f32[32,128]{1,0:T(8,128)S(1)} %get-tuple-element.361), channel_id=1, replica_groups=mesh['src'=16,'tgt'=32] {'src'}, use_global_device_ids=true, to_apply=%region_30.35 | all-reduce | flops 4096 | bytes 32768 | tf_op jit(solution)/shard_map/pmax | solution.py:42
  1094.2 55.7 %psum.45 = f32[32,128]{1,0:T(8,128)S(1)} all-reduce(f32[32,128]{1,0:T(8,128)S(1)} %exponential_multiply_fusion.1), channel_id=1, replica_groups=mesh['src'=16,'tgt'=32] {'src'}, use_global_device_ids=true, to_apply=%region_31.36 | all-reduce | flops 4096 | bytes 32768 | tf_op jit(solution)/shard_map/psum | solution.py:43
  1149.9 65.6 %while.82 = (s32[]{:T(128)}, f32[64,128]{1,0:T(8,128)S(1)}, f32[64,128]{1,0:T(8,128)S(1)}, s32[]{:T(128)}, s32[80]{0:T(128)S(1)}, /*index=5*/s32[]{:T(128)}, s32...) while((s32[]{:T(128)}, f32[64,128]{1,0:T(8,128)S(1)}, ...), condition=%wide.region_37.42_spmd.clone, body=%wide.region_32.41_spmd.clone.sunk | while | flops 69159056 | bytes 4675703 | solution.py:96
  1215.6 123.8 %pmax.46 = bf16[64,128]{1,0:T(8,128)(2,1)S(1)} all-reduce(bf16[64,128]{1,0:T(8,128)(2,1)S(1)} %convert_element_type.96), channel_id=1, replica_groups=mesh['src'=16,'tgt'=32] {'tgt'}, use_global_device_ids=true, to_apply=%region_38.43 | all-reduce | flops 8192 | bytes 32768 | tf_op jit(solution)/shard_map/pmax | solution.py:34
  1339.4 123.8 %psum.46 = bf16[64,128]{1,0:T(8,128)(2,1)S(1)} all-reduce(bf16[64,128]{1,0:T(8,128)(2,1)S(1)} %fusion.88), channel_id=1, replica_groups=mesh['src'=16,'tgt'=32] {'tgt'}, use_global_device_ids=true, to_apply=%region_39.44 | all-reduce | flops 8192 | bytes 32768 | tf_op jit(solution)/shard_map/psum | solution.py:35
  1463.3 64.9 %while.83 = (s32[]{:T(128)}, f32[32,128]{1,0:T(8,128)S(1)}, f32[32,128]{1,0:T(8,128)S(1)}, s32[]{:T(128)}, s32[80]{0:T(128)S(1)}, /*index=5*/s32[]{:T(128)}, s32...) while((s32[]{:T(128)}, f32[32,128]{1,0:T(8,128)S(1)}, ...), condition=%wide.region_45.50_spmd.clone, body=%wide.region_40.49_spmd.clone.sunk | while | flops 68920976 | bytes 4461943 | solution.py:113
  1466.2 2.8 gather_fusion.16
  1473.5 2.8 gather_fusion.16
  1480.7 2.8 gather_fusion.16
  1487.9 2.8 gather_fusion.16
  1495.1 2.8 gather_fusion.16
  1502.3 2.8 gather_fusion.16
  1509.5 2.8 gather_fusion.16
  1516.8 2.8 gather_fusion.16
  1528.3 64.8 %pmax.47 = f32[32,128]{1,0:T(8,128)S(1)} all-reduce(f32[32,128]{1,0:T(8,128)S(1)} %get-tuple-element.365), channel_id=1, replica_groups=mesh['src'=16,'tgt'=32] {'src'}, use_global_device_ids=true, to_apply=%region_46.51 | all-reduce | flops 4096 | bytes 32768 | tf_op jit(solution)/shard_map/pmax | solution.py:42
  1593.0 55.7 %psum.47 = f32[32,128]{1,0:T(8,128)S(1)} all-reduce(f32[32,128]{1,0:T(8,128)S(1)} %exponential_multiply_fusion), channel_id=1, replica_groups=mesh['src'=16,'tgt'=32] {'src'}, use_global_device_ids=true, to_apply=%region_47.52 | all-reduce | flops 4096 | bytes 32768 | tf_op jit(solution)/shard_map/psum | solution.py:43
  (937 shorter events, 317.9 us)
Async XLA Ops:
  7.2 80.2 %all-gather.5.cloned.1.call-start = ((), (), s32[]{:S(2)}) async-start(), calls=%async_computation.1 | async-start | bytes 2228224 | tf_op jit(solution)/shard_map/all_gather | solution.py:53
  7.9 140.9 %all-gather.3.cloned.1.call-start = ((), (), s32[]{:S(2)}) async-start(), calls=%async_computation | async-start | bytes 4325376 | tf_op jit(solution)/shard_map/all_gather | solution.py:49
Sparse Core Ops, SparseCore 0:
  10.1 77.2 all-gather.4
  90.5 58.2 all-gather.2
where the time goes:
time: 1660 us
  blocking collectives  1170 us (70%)
  local copies, waits for them, and re-layouts  299 us (18%)
  waiting for transfers between devices  82 us (5%)
  other arithmetic  67.8 us (4%)
  matrix products  21.6 us (1%)
    pmax x3, blocking collectives, settle_rows(): highest = lax.pmax(peaks.astype(jnp.bfloat16), 'tgt').astype(peaks.dtype)  374 us
    psum x3, blocking collectives, settle_rows(): lax.psum((totals * jnp.exp(peaks - highest)).astype(jnp.bfloat16), 'tgt')  371 us
    pmax x3, blocking collectives, settle_cols(): highest = lax.pmax(peaks, 'src')  195 us
    psum x3, blocking collectives, settle_cols(): summed = lax.psum(totals * jnp.exp(peaks - highest), 'src')  167 us
    gather x54, local copies, waits for them, and re-layouts, tile_block(): left_rows = jnp.take(sources, row_ids, axis=0)  149 us
    gather x54, local copies, waits for them, and re-layouts, tile_block(): right_rows = jnp.take(targets, col_ids, axis=0)  117 us
    all_gather x1, waiting for transfers between devices, shards(): lax.all_gather(src_points, 'tgt', axis=1, tiled=True)  61.4 us
    lt x54, other arithmetic, group_tiles(): first_slot + jnp.arange(slot_group, dtype=jnp.int32) < live_count  35.3 us
  transfers between devices with their start and end apart: 2, of which 2 were waited for; matrix products, arithmetic and copies ran while one was open for 0% of the time, Pallas kernels for 0%

commit v1 on v0

v1 whole, which is shorter than its diff:
```python
import math

import jax
import jax.numpy as jnp
from jax import lax
from jax.experimental import pallas as pl
from jax.experimental.pallas import tpu as pltpu
from jax.sharding import PartitionSpec as P

MESH = pl.DeviceIdType.MESH
TILE = 128
D = 256
ROW_TILES = 64
COL_TILES = 32
SLOTS = 80
FIXED = 64
EXTRA = SLOTS - FIXED
ITERS = 3
NS = 16
NT = 32
CHIPS = 16
HALF = ROW_TILES // 2
LOG2E = math.log2(math.e)
LN2 = math.log(2.0)
SCALE = -20.0 * LOG2E
LOWEST = -1.0e30
NT_DIMS = (((1,), (1,)), ((), ()))


def scaled_cost(left, right):
    products = lax.dot_general(left, right, NT_DIMS, preferred_element_type=jnp.float32)
    return (1.0 - products).astype(jnp.bfloat16).astype(jnp.float32) * SCALE


def peak_and_sum(scores):
    peak = jnp.max(scores, axis=0, keepdims=True)
    return peak, jnp.sum(jnp.exp2(scores - peak), axis=0, keepdims=True)


def lse_leading(parts):
    peak = jnp.max(parts, axis=0)
    return peak + jnp.log2(jnp.sum(jnp.exp2(parts - peak[None]), axis=0))


def kernel(
    xp, am, yp, bm, tiles, count, s_out, t_out,
    X, Y, A, AT, a_parts, b_parts, a_all, b_all, own_a, own_b,
    peak_r, sum_r, peak_x, sum_x, s_pot, t_pot, l_row, half_in, half_out, row_in,
    col_out, col_in, fin_out, fin_in,
    z_up, z_dn, z_send, x_recv, sib_recv, x_send, mass_recv, mass_send,
    half_recv, half_send, row_recv, row_send, col_recv, col_send,
):
    i = lax.axis_index("src")
    k = lax.axis_index("tgt")
    chip = k // 2
    core = lax.rem(k, 2)
    sibling = k + 1 - 2 * core
    up = lax.rem(i + 1, NS)
    dn = lax.rem(i + NS - 1, NS)

    barrier = pltpu.get_barrier_semaphore()

    def greet_plane(d, c):
        pl.semaphore_signal(barrier, inc=1, device_id=(i, lax.rem(k + d, NT)), device_id_type=MESH)
        return c

    def greet_line(d, c):
        pl.semaphore_signal(barrier, inc=1, device_id=(lax.rem(i + d, NS), k), device_id_type=MESH)
        return c

    lax.fori_loop(1, NT, greet_plane, 0)
    lax.fori_loop(1, NS, greet_line, 0)
    pl.semaphore_wait(barrier, NT - 1 + NS - 1)

    def remote(src, dst, ssem, rsem, dev):
        return pltpu.make_async_remote_copy(
            src_ref=src, dst_ref=dst, send_sem=ssem, recv_sem=rsem, device_id=dev, device_id_type=MESH
        )

    def drain(like, sem):
        pltpu.make_async_copy(like, like, sem).wait()

    def z_copy(src, shard, q, step, direction):
        tile = 2 * shard + q // 2
        dst = Y.at[tile, lax.rem(q, 2)]
        if src is None:
            src = dst
        if direction == 0:
            return remote(src, dst, z_send.at[0], z_up.at[step * 4 + q], (up, k))
        return remote(src, dst, z_send.at[1], z_dn.at[step * 4 + q], (dn, k))

    for q in range(4):
        for direction in range(2):
            z_copy(yp.at[q // 2, pl.ds((q % 2) * 64, 64)], i, q, 0, direction).start()
    sib_dev = (i, sibling)
    remote(xp, X.at[pl.ds(2 * k, 2)], x_send.at[1], sib_recv.at[0], sib_dev).start()

    def send_x(d, c):
        to = 2 * lax.rem(chip + d, CHIPS) + core
        remote(xp, X.at[pl.ds(2 * k, 2)], x_send.at[0], x_recv.at[d], (i, to)).start()
        return c

    lax.fori_loop(1, CHIPS, send_x, 0)

    own_a[0:1, :] = am[:, 0:TILE].astype(jnp.float32) * LOG2E
    own_a[1:2, :] = am[:, TILE:].astype(jnp.float32) * LOG2E
    own_b[0:1, :] = bm[:, 0:TILE].astype(jnp.float32) * LOG2E
    own_b[1:2, :] = bm[:, TILE:].astype(jnp.float32) * LOG2E

    def send_a(d, c):
        remote(own_a, a_parts.at[k], mass_send.at[0], mass_recv.at[0], (i, lax.rem(k + d, NT))).start()
        return c

    def send_b(d, c):
        remote(own_b, b_parts.at[i], mass_send.at[1], mass_recv.at[1], (lax.rem(i + d, NS), k)).start()
        return c

    lax.fori_loop(1, NT, send_a, 0)
    lax.fori_loop(1, NS, send_b, 0)
    a_parts[k] = own_a[...]
    b_parts[i] = own_b[...]
    X[pl.ds(2 * k, 2)] = xp[...]
    Y[pl.ds(2 * i, 2)] = yp[...].reshape(2, 2, 64, D)

    def serve_x(d):
        theirs = 2 * lax.rem(chip + CHIPS - d, CHIPS) + core
        block = X.at[pl.ds(2 * theirs, 2)]
        drain(block, x_recv.at[d])
        remote(block, block, x_send.at[1], sib_recv.at[d], sib_dev).start()

    def wait_sib(d, c):
        theirs = 2 * lax.rem(chip + CHIPS - d, CHIPS) + 1 - core
        block = X.at[pl.ds(2 * theirs, 2)]
        drain(block, sib_recv.at[d])
        return c

    def ring_step(step, c):
        lo = lax.rem(i + NS - step, NS)
        hi = lax.rem(i + step, NS)
        for q in range(4):
            for direction, shard in ((0, lo), (1, hi)):
                mine = Y.at[2 * shard + q // 2, q % 2]
                sem = (z_up, z_dn)[direction].at[(step - 1) * 4 + q]
                drain(mine, sem)
                z_copy(None, shard, q, step, direction).start()
        serve_x(2 * step - 1)
        serve_x(2 * step)
        return c

    lax.fori_loop(1, 7, ring_step, 0)
    lo = lax.rem(i + NS - 7, NS)
    hi = lax.rem(i + 7, NS)
    for q in range(4):
        for direction, shard in ((0, lo), (1, hi)):
            drain(Y.at[2 * shard + q // 2, q % 2], (z_up, z_dn)[direction].at[6 * 4 + q])
            if q // 2 == direction:
                z_copy(None, shard, q, 7, direction).start()
    for d in (13, 14, 15):
        serve_x(d)
    far = lax.rem(i + 8, NS)
    for q in range(4):
        drain(Y.at[2 * far + q // 2, q % 2], (z_up, z_dn)[q // 2].at[7 * 4 + q])
    lax.fori_loop(0, CHIPS, wait_sib, 0)
    drain(a_parts.at[pl.ds(0, NT - 1)], mass_recv.at[0])
    drain(b_parts.at[pl.ds(0, NS - 1)], mass_recv.at[1])

    def lay_a(n, c):
        for h in range(2):
            a_all[pl.ds(2 * n + h, 1), :] = a_parts[n, h : h + 1]
        return c

    def lay_b(n, c):
        for h in range(2):
            b_all[pl.ds(2 * n + h, 1), :] = b_parts[n, h : h + 1]
        return c

    lax.fori_loop(0, NT, lay_a, 0)
    lax.fori_loop(0, NS, lay_b, 0)

    def fixed_tiles(c, carry):
        y = Y[c].reshape(TILE, D)
        for h in range(2):
            r = c + COL_TILES * h
            x = X[r]
            costs = scaled_cost(y, x)
            AT[r] = costs
            peak, total = peak_and_sum(costs)
            peak_r[pl.ds(r, 1), :] = peak
            sum_r[pl.ds(r, 1), :] = total
            A[r] = scaled_cost(x, y)
        return carry

    lax.fori_loop(0, COL_TILES, fixed_tiles, 0)

    live_count = count[0]

    def alive(s):
        return jnp.full((1, TILE), live_count, jnp.int32) > FIXED + s

    def keep_extra(s, peak, total):
        peak_x[pl.ds(s, 1), :] = jnp.where(alive(s), peak, LOWEST)
        sum_x[pl.ds(s, 1), :] = total

    def extra_tiles(s, carry):
        x = X[tiles[2 * (FIXED + s)]]
        y = Y[tiles[2 * (FIXED + s) + 1]].reshape(TILE, D)
        costs = scaled_cost(y, x)
        AT[FIXED + s] = costs
        keep_extra(s, *peak_and_sum(costs))
        A[FIXED + s] = scaled_cost(x, y)
        return carry

    lax.fori_loop(0, EXTRA, extra_tiles, 0)

    def fold(peak, total, which):
        owner = lax.broadcasted_iota(jnp.int32, peak.shape, 0)
        px = peak_x[...]
        sx = sum_x[...]
        highest = peak
        for s in range(EXTRA):
            mine = owner == tiles[2 * (FIXED + s) + which]
            highest = jnp.maximum(highest, jnp.where(mine, px[s : s + 1], LOWEST))
        total = total * jnp.exp2(peak - highest)
        for s in range(EXTRA):
            mine = owner == tiles[2 * (FIXED + s) + which]
            shortfall = jnp.minimum(px[s : s + 1] - highest, 0.0)
            total = total + jnp.where(mine, sx[s : s + 1] * jnp.exp2(shortfall), 0.0)
        return highest + jnp.log2(total)

    def columns_of(pot):
        rows = pot.shape[0]
        full = jnp.concatenate([pot, jnp.zeros((TILE - rows, TILE), jnp.float32)], axis=0)
        return full.T

    def pick(cols, n):
        lane = lax.broadcasted_iota(jnp.int32, (TILE, TILE), 1)
        return jnp.sum(jnp.where(lane == n, cols, 0.0), axis=1, keepdims=True)

    def row_pass():
        cols = columns_of(t_pot[...])

        def group(g, carry):
            near = pltpu.roll(cols, lax.rem(TILE - 8 * g, TILE), 1)
            for u in range(8):
                pot = near[:, u : u + 1]
                for h in range(2):
                    r = 8 * g + u + COL_TILES * h
                    peak, total = peak_and_sum(AT[r] + pot)
                    peak_r[pl.ds(r, 1), :] = peak
                    sum_r[pl.ds(r, 1), :] = total
            return carry

        lax.fori_loop(0, COL_TILES // 8, group, 0)

        def extra(s, carry):
            pot = pick(cols, tiles[2 * (FIXED + s) + 1])
            keep_extra(s, *peak_and_sum(AT[FIXED + s] + pot))
            return carry

        lax.fori_loop(0, EXTRA, extra, 0)

    def col_pass():
        cols = columns_of(s_pot[...])

        def group(g, carry):
            near = pltpu.roll(cols, lax.rem(TILE - 8 * g, TILE), 1)
            for u in range(8):
                c = 8 * g + u
                first = A[c] + near[:, u : u + 1]
                second = A[c + COL_TILES] + near[:, COL_TILES + u : COL_TILES + u + 1]
                peak, total = peak_and_sum(jnp.concatenate([first, second], axis=0))
                peak_r[pl.ds(c, 1), :] = peak
                sum_r[pl.ds(c, 1), :] = total
            return carry

        lax.fori_loop(0, COL_TILES // 8, group, 0)

        def extra(s, carry):
            pot = pick(cols, tiles[2 * (FIXED + s)])
            keep_extra(s, *peak_and_sum(A[FIXED + s] + pot))
            return carry

        lax.fori_loop(0, EXTRA, extra, 0)

    for it in range(ITERS):
        if it > 0:
            row_pass()
        logs = fold(peak_r[...], sum_r[...], 0)
        l_row[it] = logs.reshape(2, HALF, TILE)
        remote(l_row.at[it, 1 - core], half_in.at[it], half_send.at[it], half_recv.at[it], sib_dev).start()
        drain(half_in.at[it], half_recv.at[it])
        one, two = l_row[it, core], half_in[it]
        top = jnp.maximum(one, two)
        both = top + jnp.log2(jnp.exp2(one - top) + jnp.exp2(two - top))
        half_out[it] = both
        row_in[it, k] = both

        def send_row(d, c):
            remote(
                half_out.at[it], row_in.at[it, k], row_send.at[it], row_recv.at[it], (i, lax.rem(k + d, NT))
            ).start()
            return c

        lax.fori_loop(1, NT, send_row, 0)
        drain(row_in.at[it, pl.ds(0, NT - 1)], row_recv.at[it])
        total = lse_leading(row_in[it].reshape(CHIPS, ROW_TILES, TILE))
        s_pot[...] = a_all[...] - total

        col_pass()
        logs = fold(peak_r[0:COL_TILES, :], sum_r[0:COL_TILES, :], 1)
        if it + 1 < ITERS:
            col_out[it] = logs
            col_in[it, i] = logs

            def send_col(d, c):
                remote(
                    col_out.at[it], col_in.at[it, i], col_send.at[it], col_recv.at[it], (lax.rem(i + d, NS), k)
                ).start()
                return c

            lax.fori_loop(0, NS - 1, lambda d, c: send_col(lax.rem(d + 8, NS - 1) + 1, c), 0)
            drain(col_in.at[it, pl.ds(0, NS - 1)], col_recv.at[it])
            t_pot[...] = b_all[...] - lse_leading(col_in[it])
    for n in range(NS):
        fin_out[n] = logs[2 * n : 2 * n + 2]
    fin_in[i] = fin_out[i]

    def send_fin(d, c):
        to = lax.rem(i + lax.rem(d + 8, NS - 1) + 1, NS)
        remote(fin_out.at[to], fin_in.at[i], col_send.at[2], col_recv.at[2], (to, k)).start()
        return c

    lax.fori_loop(0, NS - 1, send_fin, 0)
    s_out[...] = s_pot[pl.ds(2 * k, 2), :] * LN2
    drain(Y.at[pl.ds(0, 15)], z_send.at[0])
    drain(Y.at[pl.ds(0, 15)], z_send.at[1])
    drain(X.at[pl.ds(0, 30)], x_send.at[0])
    drain(X.at[pl.ds(0, 32)], x_send.at[1])
    drain(a_parts.at[pl.ds(0, NT - 1)], mass_send.at[0])
    drain(b_parts.at[pl.ds(0, NS - 1)], mass_send.at[1])
    for it in range(ITERS):
        drain(half_in.at[it], half_send.at[it])
        drain(row_in.at[it, pl.ds(0, NT - 1)], row_send.at[it])
        if it + 1 < ITERS:
            drain(col_in.at[it, pl.ds(0, NS - 1)], col_send.at[it])
    drain(fin_in.at[pl.ds(0, NS - 1)], col_send.at[2])
    drain(fin_in.at[pl.ds(0, NS - 1)], col_recv.at[2])
    t_out[...] = (own_b[...] - lse_leading(fin_in[...])) * LN2


def shards(src_points, src_logmass, tgt_points, tgt_logmass, tile_list, tile_count):
    f32, bf16 = jnp.float32, jnp.bfloat16
    vmem = pl.BlockSpec(memory_space=pltpu.VMEM)
    smem = pl.BlockSpec(memory_space=pltpu.SMEM)
    dma = pltpu.SemaphoreType.DMA
    s, t = pl.pallas_call(
        kernel,
        out_shape=(
            jax.ShapeDtypeStruct((2, TILE), f32),
            jax.ShapeDtypeStruct((2, TILE), f32),
        ),
        in_specs=[vmem, vmem, vmem, vmem, smem, smem],
        out_specs=(vmem, vmem),
        scratch_shapes=[
            pltpu.VMEM((ROW_TILES, TILE, D), bf16),
            pltpu.VMEM((COL_TILES, 2, 64, D), bf16),
            pltpu.VMEM((SLOTS, TILE, TILE), f32),
            pltpu.VMEM((SLOTS, TILE, TILE), f32),
            pltpu.VMEM((NT, 2, TILE), f32),
            pltpu.VMEM((NS, 2, TILE), f32),
            pltpu.VMEM((ROW_TILES, TILE), f32),
            pltpu.VMEM((COL_TILES, TILE), f32),
            pltpu.VMEM((2, TILE), f32),
            pltpu.VMEM((2, TILE), f32),
            pltpu.VMEM((ROW_TILES, TILE), f32),
            pltpu.VMEM((ROW_TILES, TILE), f32),
            pltpu.VMEM((EXTRA, TILE), f32),
            pltpu.VMEM((EXTRA, TILE), f32),
            pltpu.VMEM((ROW_TILES, TILE), f32),
            pltpu.VMEM((COL_TILES, TILE), f32),
            pltpu.VMEM((ITERS, 2, HALF, TILE), f32),
            pltpu.VMEM((ITERS, HALF, TILE), f32),
            pltpu.VMEM((ITERS, HALF, TILE), f32),
            pltpu.VMEM((ITERS, NT, HALF, TILE), f32),
            pltpu.VMEM((ITERS - 1, COL_TILES, TILE), f32),
            pltpu.VMEM((ITERS - 1, NS, COL_TILES, TILE), f32),
            pltpu.VMEM((NS, 2, TILE), f32),
            pltpu.VMEM((NS, 2, TILE), f32),
            dma((32,)),
            dma((32,)),
            dma((2,)),
            dma((CHIPS,)),
            dma((CHIPS,)),
            dma((2,)),
            dma((2,)),
            dma((2,)),
            dma((ITERS,)),
            dma((ITERS,)),
            dma((ITERS,)),
            dma((ITERS,)),
            dma((ITERS,)),
            dma((ITERS,)),
        ],
        compiler_params=pltpu.CompilerParams(
            collective_id=0, has_side_effects=True, vmem_limit_bytes=50 * 2**20
        ),
    )(
        src_points.reshape(2, TILE, D),
        src_logmass,
        tgt_points.reshape(2, TILE, D),
        tgt_logmass,
        tile_list.reshape(2 * SLOTS),
        tile_count.reshape(1),
    )
    return s.reshape(1, 2 * TILE), t.reshape(1, 2 * TILE)


def solution(mesh):
    placed = (
        P("src", "tgt", None),
        P("src", "tgt"),
        P("tgt", "src", None),
        P("tgt", "src"),
        P("src", "tgt", None, None),
        P("src", "tgt"),
    )
    return jax.shard_map(
        shards,
        mesh=mesh,
        in_specs=placed,
        out_specs=(P("src", "tgt"), P("tgt", "src")),
        check_vma=False,
    )
```

time: 1660 us -> 178 us (0.11)
  the two profiles are of different devices: /device:TPU:32 before, /device:TPU:1 now
where the time goes in v1:
time: 178 us
  Pallas kernels  172 us (97%)
  local copies, waits for them, and re-layouts  4.52 us (3%)
    pallas_call x1, Pallas kernels, shards(): pl.pallas_call(kernel, out_shape=(jax.ShapeDtypeStruct((2, TILE), f32), j...  172 us
    unnamed x11, local copies, waits for them, and re-layouts  4.39 us

profile of v1, /device:TPU:1, one launch (start us, length us, event | category | flops | bytes accessed | tf_op | source)
XLA Modules:
  0.0 178.0 jit_solution(9559707193258889505)
XLA Ops:
  0.6 0.8 copy.8
  1.4 0.1 reshape.24.tiles
  2.2 0.0 copy-start.3
  2.2 0.0 copy-start.2
  2.2 0.7 copy-done.3
  2.9 0.0 copy-done.2
  2.9 0.0 copy-start
  2.9 0.9 copy-done
  3.8 0.0 copy-start.1
  3.8 0.9 copy-done.1
  4.7 172.1 %shard_map.77 = (f32[2,128]{1,0:T(2,128)S(1)}, f32[2,128]{1,0:T(2,128)S(1)}) custom-call(bf16[2,128,256]{2,1,0:T(8,128)(2,1)S(1)} %bitcast.8, bf16[1,256]{1,0:T(2,128)(2,1)S(1)} %copy-done.2, bf16[2,128,256]{2,1,0:T(8,128)(2,1)S(1)} %bitcast.9, bf16[1,256]{1,0:T(2,128)(2,1)S(1)} %copy-done.3, s32[160]{0:T(256)S(1)} %reshape.24.tiles, s32[1]{0:T(128)} %bitcast.7.count), custom_call_target="tpu_custom_call" | custom-call | tf_op jit(solution)/shard_map/pallas_call | solution.py:356
  176.8 0.6 copy.12
  177.4 0.6 copy.13
Async XLA Ops:
  2.2 0.7 copy-start.3
  2.2 0.7 copy-start.2
  2.9 0.9 copy-start
  3.8 0.9 copy-start.1

commit v2 on v1

v2 whole, which is shorter than its diff:
```python
import math

import jax
import jax.numpy as jnp
from jax import lax
from jax.experimental import pallas as pl
from jax.experimental.pallas import tpu as pltpu
from jax.sharding import PartitionSpec as P

MESH = pl.DeviceIdType.MESH
TILE = 128
D = 256
ROW_TILES = 64
COL_TILES = 32
SLOTS = 80
FIXED = 64
EXTRA = SLOTS - FIXED
ITERS = 3
NS = 16
NT = 32
HALF = ROW_TILES // 2
LOG2E = math.log2(math.e)
LN2 = math.log(2.0)
SCALE = -20.0 * LOG2E
LOWEST = -1.0e30
NT_DIMS = (((1,), (1,)), ((), ()))


def scaled_cost(left, right):
    products = lax.dot_general(left, right, NT_DIMS, preferred_element_type=jnp.float32)
    return (1.0 - products).astype(jnp.bfloat16).astype(jnp.float32) * SCALE


def peak_and_sum(scores):
    peak = jnp.max(scores, axis=0, keepdims=True)
    return peak, jnp.sum(jnp.exp2(scores - peak), axis=0, keepdims=True)


def lse_leading(parts):
    peak = jnp.max(parts, axis=0)
    return peak + jnp.log2(jnp.sum(jnp.exp2(parts - peak[None]), axis=0))


def kernel(
    xp, am, yp, bm, tiles, count, s_out, t_out,
    X, Y, A, AT, a_parts, b_parts, a_all, b_all, own_a, own_b,
    peak_r, sum_r, peak_x, sum_x, s_pot, t_pot, row_tot, col_tot,
    half_out, half_in, row_out, row_in, row_out16, row_in16,
    col_out, col_in, col_out16, col_in16, fin_out, fin_in,
    z_up, z_dn, z_send, xa, xb, x_send, sib_recv, mass_recv, mass_send, local,
    half_recv, half_send, row_recv, row_send, col_recv, col_send,
):
    i = lax.axis_index("src")
    k = lax.axis_index("tgt")
    core = lax.rem(k, 2)
    sibling = k + 1 - 2 * core
    up = lax.rem(i + 1, NS)
    dn = lax.rem(i + NS - 1, NS)
    px, py = k // 8, lax.rem(k // 2, 4)
    pa = px * (1 - core) + py * core
    pb = py * (1 - core) + px * core

    def at(da, db):
        a, b = lax.rem(pa + 4 + da, 4), lax.rem(pb + 4 + db, 4)
        return (a * (1 - core) + b * core) * 8 + (b * (1 - core) + a * core) * 2 + core

    barrier = pltpu.get_barrier_semaphore()
    near = ((up, k), (dn, k), (i, at(1, 0)), (i, at(-1, 0)), (i, at(0, 1)), (i, at(0, -1)), (i, sibling))
    for dev in near:
        pl.semaphore_signal(barrier, inc=1, device_id=dev, device_id_type=MESH)
    own_x = pltpu.make_async_copy(xp, X.at[pl.ds(2 * k, 2)], local.at[0])
    own_y = pltpu.make_async_copy(yp, Y.at[pl.ds(2 * i, 2)], local.at[1])
    own_x.start()
    own_y.start()
    own_x.wait()
    own_y.wait()
    pl.semaphore_wait(barrier, len(near))

    def remote(src, dst, ssem, rsem, dev):
        return pltpu.make_async_remote_copy(
            src_ref=src, dst_ref=dst, send_sem=ssem, recv_sem=rsem, device_id=dev, device_id_type=MESH
        )

    def drain(like, sem):
        pltpu.make_async_copy(like, like, sem).wait()

    def z_copy(shard, q, step, direction):
        block = Y.at[2 * shard + q // 2, pl.ds((q % 2) * 64, 64)]
        if direction == 0:
            return remote(block, block, z_send.at[0], z_up.at[step * 4 + q], (up, k))
        return remote(block, block, z_send.at[1], z_dn.at[step * 4 + q], (dn, k))

    def z_wait(shard, q, step, direction):
        drain(Y.at[2 * shard + q // 2, pl.ds((q % 2) * 64, 64)], (z_up, z_dn)[direction].at[step * 4 + q])

    def x_block(da, db):
        return X.at[pl.ds(2 * at(da, db), 2)]

    def x_tile(da, db, t):
        return X.at[2 * at(da, db) + t]

    def x_copy(block, sem, da, db):
        remote(block, block, x_send.at[0], sem, (i, at(da, db))).start()

    def x_sibling(da, db):
        block = x_block(da, db)
        remote(block, block, x_send.at[1], sib_recv.at[0], (i, sibling)).start()

    OFFSETS = (0, -1, 1, 2)

    def x_both(j):
        block = x_block(OFFSETS[j], 0)
        x_copy(block, xb.at[j], 0, 1)
        x_copy(block, xb.at[4 + j], 0, -1)
        x_sibling(OFFSETS[j], 0)

    def x_step(step):
        if step == 1:
            for j, da, tile in ((1, -1, 0), (2, 1, 1)):
                drain(x_block(da, 0), xa.at[j - 1])
                x_copy(x_tile(da, 0, tile), xa.at[1 + j], -da, 0)
                x_both(j)
        if step == 2:
            drain(x_tile(2, 0, 0), xa.at[2])
            drain(x_tile(2, 0, 1), xa.at[3])
            x_both(3)
        for j in {2: (0,), 3: (1, 2), 4: (3,)}.get(step, ()):
            for n, db in ((0, -1), (1, 1)):
                drain(x_block(OFFSETS[j], db), xb.at[4 * n + j])
                x_copy(x_tile(OFFSETS[j], db, n), xb.at[8 + 4 * n + j], 0, -db)
                x_sibling(OFFSETS[j], db)
        for j in {4: (0,), 5: (1, 2, 3)}.get(step, ()):
            for n in range(2):
                drain(x_tile(OFFSETS[j], 2, n), xb.at[8 + 4 * n + j])
            x_sibling(OFFSETS[j], 2)
        if step == 6:
            drain(X.at[pl.ds(0, 2 * NS)], sib_recv.at[0])

    def shard_costs(n, carry):
        shard = lax.rem(i + n, NS)
        for half in range(2):
            c = 2 * shard + half
            y = Y[c]
            for h in range(2):
                r = c + COL_TILES * h
                costs = scaled_cost(y, X[r])
                AT[r] = costs
                peak, total = peak_and_sum(costs)
                peak_r[pl.ds(r, 1), :] = peak
                sum_r[pl.ds(r, 1), :] = total
        return carry

    for q in range(4):
        for direction in range(2):
            z_copy(i, q, 0, direction).start()
    x_copy(x_block(0, 0), xa.at[0], 1, 0)
    x_copy(x_block(0, 0), xa.at[1], -1, 0)
    x_both(0)
    own_a[0:1, :] = am[:, 0:TILE].astype(jnp.float32) * LOG2E
    own_a[1:2, :] = am[:, TILE:].astype(jnp.float32) * LOG2E
    own_b[0:1, :] = bm[:, 0:TILE].astype(jnp.float32) * LOG2E
    own_b[1:2, :] = bm[:, TILE:].astype(jnp.float32) * LOG2E
    a_parts[k] = own_a[...]
    b_parts[i] = own_b[...]
    for step in range(1, 8):
        lo = lax.rem(i + NS - step, NS)
        hi = lax.rem(i + step, NS)
        for q in range(4):
            for direction, shard in ((0, lo), (1, hi)):
                z_wait(shard, q, step - 1, direction)
                if step < 7 or q // 2 == direction:
                    z_copy(shard, q, step, direction).start()
        x_step(step)
        if step == 6:
            lax.fori_loop(NS - 3, NS + 4, shard_costs, 0)
        if step == 7:
            lax.fori_loop(NS - 6, NS - 3, shard_costs, 0)
            lax.fori_loop(4, 7, shard_costs, 0)
    far = lax.rem(i + 8, NS)
    for q in range(4):
        z_wait(far, q, 7, q // 2)
    lax.fori_loop(7, 10, shard_costs, 0)
    live_count = count[0, 0]

    def alive(s):
        return jnp.full((1, TILE), live_count, jnp.int32) > FIXED + s

    def keep_extra(s, peak, total):
        peak_x[pl.ds(s, 1), :] = jnp.where(alive(s), peak, LOWEST)
        sum_x[pl.ds(s, 1), :] = total

    def row_of(s):
        return tiles[0, FIXED + s]

    def col_of(s):
        return tiles[1, FIXED + s]

    def grouped(body, count, size):
        def group(g, carry):
            for u in range(size):
                body(size * g + u)
            return carry

        lax.fori_loop(0, count // size, group, 0)

    def extra_first(s):
        costs = scaled_cost(Y[col_of(s)], X[row_of(s)])
        AT[FIXED + s] = costs
        keep_extra(s, *peak_and_sum(costs))

    def extra_second(s):
        A[FIXED + s] = scaled_cost(X[row_of(s)], Y[col_of(s)])

    def fixed_second(c):
        for h in range(2):
            r = c + COL_TILES * h
            A[r] = scaled_cost(X[r], Y[c])

    def fold(first, which):
        peak = peak_r[pl.ds(first, HALF), :]
        owner = lax.broadcasted_iota(jnp.int32, (HALF, TILE), 0) + first
        pick_id = row_of if which == 0 else col_of
        px = peak_x[...]
        sx = sum_x[...]
        highest = peak
        for s in range(EXTRA):
            highest = jnp.maximum(highest, jnp.where(owner == pick_id(s), px[s : s + 1], LOWEST))
        total = sum_r[pl.ds(first, HALF), :] * jnp.exp2(peak - highest)
        for s in range(EXTRA):
            shortfall = jnp.minimum(px[s : s + 1] - highest, 0.0)
            total = total + jnp.where(owner == pick_id(s), sx[s : s + 1] * jnp.exp2(shortfall), 0.0)
        return highest + jnp.log2(total)

    def columns_of(pot):
        rows = pot.shape[0]
        full = jnp.concatenate([pot, jnp.zeros((TILE - rows, TILE), jnp.float32)], axis=0)
        return full.T

    def pick(cols, n):
        lane = lax.broadcasted_iota(jnp.int32, (TILE, TILE), 1)
        return jnp.sum(jnp.where(lane == n, cols, 0.0), axis=1, keepdims=True)

    def row_extras(cols):
        grouped(lambda s: keep_extra(s, *peak_and_sum(AT[FIXED + s] + pick(cols, col_of(s)))), EXTRA, 4)

    def row_half(cols, first):
        def group(g, carry):
            near = pltpu.roll(cols, lax.rem(TILE - 8 * g, TILE), 1)
            for u in range(8):
                r = 8 * g + u + first
                peak, total = peak_and_sum(AT[r] + near[:, u : u + 1])
                peak_r[pl.ds(r, 1), :] = peak
                sum_r[pl.ds(r, 1), :] = total
            return carry

        lax.fori_loop(0, HALF // 8, group, 0)

    def col_pass():
        cols = columns_of(s_pot[...])

        def group(g, carry):
            near = pltpu.roll(cols, lax.rem(TILE - 8 * g, TILE), 1)
            for u in range(8):
                c = 8 * g + u
                first = A[c] + near[:, u : u + 1]
                second = A[c + COL_TILES] + near[:, COL_TILES + u : COL_TILES + u + 1]
                peak, total = peak_and_sum(jnp.concatenate([first, second], axis=0))
                peak_r[pl.ds(c, 1), :] = peak
                sum_r[pl.ds(c, 1), :] = total
            return carry

        lax.fori_loop(0, COL_TILES // 8, group, 0)
        grouped(lambda s: keep_extra(s, *peak_and_sum(A[FIXED + s] + pick(cols, row_of(s)))), EXTRA, 4)

    def to_plane(src, dst, ssem, rsem):
        def send(d, c):
            remote(src, dst, ssem, rsem, (i, lax.rem(k + d, NT))).start()
            return c

        lax.fori_loop(1, NT, send, 0)

    def to_line(src, dst, ssem, rsem):
        def send(d, c):
            to = lax.rem(i + lax.rem(d + 6, NS - 1) + 1, NS)
            remote(src, dst, ssem, rsem, (to, k)).start()
            return c

        lax.fori_loop(0, NS - 1, send, 0)

    mine = pl.multiple_of(HALF * core, HALF)
    other = HALF - mine
    grouped(extra_first, EXTRA, 4)
    for it in range(ITERS):
        if it > 0:
            cols = columns_of(t_pot[...])
            row_extras(cols)
            row_half(cols, other)
        half_out[it] = fold(other, 0)
        remote(half_out.at[it], half_in.at[it], half_send.at[it], half_recv.at[it], (i, sibling)).start()
        if it > 0:
            row_half(cols, mine)
        one = fold(mine, 0)
        drain(half_in.at[it], half_recv.at[it])
        two = half_in[it]
        top = jnp.maximum(one, two)
        both = top + jnp.log2(jnp.exp2(one - top) + jnp.exp2(two - top))
        if it == 0:
            row_out[...] = both
            row_in[k] = both
            to_plane(row_out, row_in.at[k], row_send.at[0], row_recv.at[0])
            to_line(own_b, b_parts.at[i], mass_send.at[1], mass_recv.at[1])
            to_plane(own_a, a_parts.at[k], mass_send.at[0], mass_recv.at[0])
            grouped(extra_second, EXTRA, 4)
            grouped(fixed_second, COL_TILES, 4)
            drain(row_in.at[pl.ds(0, NT - 1)], row_recv.at[0])
            total = lse_leading(row_in[...].reshape(NS, ROW_TILES, TILE))
            drain(a_parts.at[pl.ds(0, NT - 1)], mass_recv.at[0])
            for n in range(NT):
                a_all[2 * n : 2 * n + 2, :] = a_parts[n]
        else:
            rest = (both - row_tot[pl.ds(mine, HALF), :]).astype(jnp.bfloat16)
            row_out16[it - 1] = rest
            row_in16[it - 1, k] = rest
            to_plane(row_out16.at[it - 1], row_in16.at[it - 1, k], row_send.at[it], row_recv.at[it])
            drain(row_in16.at[it - 1, pl.ds(0, NT - 1)], row_recv.at[it])
            parts = row_in16[it - 1].reshape(NS, ROW_TILES, TILE).astype(jnp.float32)
            total = row_tot[...] + lse_leading(parts)
        row_tot[...] = total
        s_pot[...] = a_all[...] - total

        col_pass()
        logs = fold(0, 1)
        if it == 0:
            col_out[...] = logs
            col_in[i] = logs
            to_line(col_out, col_in.at[i], col_send.at[0], col_recv.at[0])
            drain(b_parts.at[pl.ds(0, NS - 1)], mass_recv.at[1])
            for n in range(NS):
                b_all[2 * n : 2 * n + 2, :] = b_parts[n]
            drain(col_in.at[pl.ds(0, NS - 1)], col_recv.at[0])
            total = lse_leading(col_in[...])
        elif it + 1 < ITERS:
            rest = (logs - col_tot[...]).astype(jnp.bfloat16)
            col_out16[...] = rest
            col_in16[i] = rest
            to_line(col_out16, col_in16.at[i], col_send.at[it], col_recv.at[it])
            drain(col_in16.at[pl.ds(0, NS - 1)], col_recv.at[it])
            total = col_tot[...] + lse_leading(col_in16[...].astype(jnp.float32))
        if it + 1 < ITERS:
            col_tot[...] = total
            t_pot[...] = b_all[...] - total
    for n in range(NS):
        fin_out[n] = logs[2 * n : 2 * n + 2]
    fin_in[i] = fin_out[i]

    def send_fin(d, c):
        to = lax.rem(i + lax.rem(d + 6, NS - 1) + 1, NS)
        remote(fin_out.at[to], fin_in.at[i], col_send.at[2], col_recv.at[2], (to, k)).start()
        return c

    lax.fori_loop(0, NS - 1, send_fin, 0)
    s_out[...] = s_pot[pl.ds(2 * k, 2), :] * LN2
    drain(Y.at[pl.ds(0, 15)], z_send.at[0])
    drain(Y.at[pl.ds(0, 15)], z_send.at[1])
    drain(X.at[pl.ds(0, 30)], x_send.at[0])
    drain(X.at[pl.ds(0, 32)], x_send.at[1])
    drain(a_parts.at[pl.ds(0, NT - 1)], mass_send.at[0])
    drain(b_parts.at[pl.ds(0, NS - 1)], mass_send.at[1])
    for it in range(ITERS):
        drain(half_in.at[it], half_send.at[it])
    drain(row_in.at[pl.ds(0, NT - 1)], row_send.at[0])
    for it in range(1, ITERS):
        drain(row_in16.at[it - 1, pl.ds(0, NT - 1)], row_send.at[it])
    drain(col_in.at[pl.ds(0, NS - 1)], col_send.at[0])
    drain(col_in16.at[pl.ds(0, NS - 1)], col_send.at[1])
    drain(fin_in.at[pl.ds(0, NS - 1)], col_send.at[2])
    drain(fin_in.at[pl.ds(0, NS - 1)], col_recv.at[2])
    t_out[...] = (own_b[...] - lse_leading(fin_in[...])) * LN2


def shards(src_points, src_logmass, tgt_points, tgt_logmass, tile_list, tile_count):
    f32, bf16 = jnp.float32, jnp.bfloat16
    vmem = pl.BlockSpec(memory_space=pltpu.VMEM)
    smem = pl.BlockSpec(memory_space=pltpu.SMEM)
    hbm = pl.BlockSpec(memory_space=pltpu.HBM)
    dma = pltpu.SemaphoreType.DMA
    s, t = pl.pallas_call(
        kernel,
        out_shape=(
            jax.ShapeDtypeStruct((2, TILE), f32),
            jax.ShapeDtypeStruct((2, TILE), f32),
        ),
        in_specs=[hbm, vmem, hbm, vmem, smem, smem],
        out_specs=(vmem, vmem),
        scratch_shapes=[
            pltpu.VMEM((ROW_TILES, TILE, D), bf16),
            pltpu.VMEM((COL_TILES, TILE, D), bf16),
            pltpu.VMEM((SLOTS, TILE, TILE), f32),
            pltpu.VMEM((SLOTS, TILE, TILE), f32),
            pltpu.VMEM((NT, 2, TILE), f32),
            pltpu.VMEM((NS, 2, TILE), f32),
            pltpu.VMEM((ROW_TILES, TILE), f32),
            pltpu.VMEM((COL_TILES, TILE), f32),
            pltpu.VMEM((2, TILE), f32),
            pltpu.VMEM((2, TILE), f32),
            pltpu.VMEM((ROW_TILES, TILE), f32),
            pltpu.VMEM((ROW_TILES, TILE), f32),
            pltpu.VMEM((EXTRA, TILE), f32),
            pltpu.VMEM((EXTRA, TILE), f32),
            pltpu.VMEM((ROW_TILES, TILE), f32),
            pltpu.VMEM((COL_TILES, TILE), f32),
            pltpu.VMEM((ROW_TILES, TILE), f32),
            pltpu.VMEM((COL_TILES, TILE), f32),
            pltpu.VMEM((ITERS, HALF, TILE), f32),
            pltpu.VMEM((ITERS, HALF, TILE), f32),
            pltpu.VMEM((HALF, TILE), f32),
            pltpu.VMEM((NT, HALF, TILE), f32),
            pltpu.VMEM((ITERS - 1, HALF, TILE), bf16),
            pltpu.VMEM((ITERS - 1, NT, HALF, TILE), bf16),
            pltpu.VMEM((COL_TILES, TILE), f32),
            pltpu.VMEM((NS, COL_TILES, TILE), f32),
            pltpu.VMEM((COL_TILES, TILE), bf16),
            pltpu.VMEM((NS, COL_TILES, TILE), bf16),
            pltpu.VMEM((NS, 2, TILE), f32),
            pltpu.VMEM((NS, 2, TILE), f32),
            dma((32,)),
            dma((32,)),
            dma((2,)),
            dma((4,)),
            dma((16,)),
            dma((2,)),
            dma((1,)),
            dma((2,)),
            dma((2,)),
            dma((2,)),
            dma((ITERS,)),
            dma((ITERS,)),
            dma((ITERS,)),
            dma((ITERS,)),
            dma((ITERS,)),
            dma((ITERS,)),
        ],
        compiler_params=pltpu.CompilerParams(
            collective_id=0, has_side_effects=True, vmem_limit_bytes=60 * 2**20
        ),
    )(
        src_points.reshape(2, TILE, D),
        src_logmass,
        tgt_points.reshape(2, TILE, D),
        tgt_logmass,
        tile_list.reshape(SLOTS, 2).T,
        tile_count,
    )
    return s.reshape(1, 2 * TILE), t.reshape(1, 2 * TILE)


def solution(mesh):
    placed = (
        P("src", "tgt", None),
        P("src", "tgt"),
        P("tgt", "src", None),
        P("tgt", "src"),
        P("src", "tgt", None, None),
        P("src", "tgt"),
    )
    return jax.shard_map(
        shards,
        mesh=mesh,
        in_specs=placed,
        out_specs=(P("src", "tgt"), P("tgt", "src")),
        check_vma=False,
    )
```

time: 178 us -> 122 us (0.69)
  Pallas kernels: 172 us -> 118 us
  local copies, waits for them, and re-layouts: 4.52 us -> 1.85 us
    pallas_call x1, Pallas kernels: 172 us -> 118 us  [shards(): pl.pallas_call(kernel, out_shape=(jax.ShapeDtypeStruct((2, TILE), f32), j...]
    unnamed x11 -> x6, local copies, waits for them, and re-layouts: 4.39 us -> 1.85 us
where the time goes in v2:
time: 122 us; the launch traced here: 121 us
  Pallas kernels  118 us (97%)
  local copies, waits for them, and re-layouts  1.85 us (2%)
  between operations  1.3 us (1%)
    pallas_call x1, Pallas kernels, shards(): pl.pallas_call(kernel, out_shape=(jax.ShapeDtypeStruct((2, TILE), f32), j...  118 us

profile of v2, /device:TPU:1, one launch (start us, length us, event | category | flops | bytes accessed | tf_op | source)
XLA Modules:
  0.0 121.4 jit_solution(3631237787405365979)
XLA Ops:
  1.3 118.2 %shard_map.77 = (f32[2,128]{1,0:T(2,128)}, f32[2,128]{1,0:T(2,128)}) custom-call(bf16[2,128,256]{2,1,0:T(8,128)(2,1)} %bitcast.7, bf16[1,256]{1,0:T(2,128)(2,1)} %am.1, bf16[2,128,256]{2,1,0:T(8,128)(2,1)} %bitcast.8, bf16[1,256]{1,0:T(2,128)(2,1)} %bm.1, s32[2,80]{1,0:T(2,128)} %bitcast.9, s32[1,1]{1,0:T(1,128)S(6)} %copy.10.count), custom_call_target="tpu_custom_call" | custom-call | tf_op jit(solution)/shard_map/pallas_call | solution.py:387
  119.5 0.0 copy-start.1
  119.5 0.7 copy-done.1
  120.2 0.0 copy-start
  120.2 0.6 copy.11
  120.8 0.1 copy-done
  120.8 0.6 copy.12
Async XLA Ops:
  119.5 0.7 copy-start.1
  120.2 0.6 copy-start

commit v3 on v2

--- a/solution.py
+++ b/solution.py
@@ -18,6 +18,13 @@
 ITERS = 3
 NS = 16
 NT = 32
+PIECES = 4
+PLANE = sorted(
+    ((x, y, c) for x in range(4) for y in range(4) for c in range(2) if x + y + c),
+    key=lambda d: -(d[0] % 4 * (4 - d[0]) + d[1] % 4 * (4 - d[1])),
+)
+PIECE = 2 * TILE // PIECES
+QUARTER = COL_TILES // 2
 HALF = ROW_TILES // 2
 LOG2E = math.log2(math.e)
 LN2 = math.log(2.0)
@@ -42,13 +49,14 @@
 
 
 def kernel(
-    xp, am, yp, bm, tiles, count, s_out, t_out,
+    xp, am, yp, bm, tiles_hbm, count_hbm, pots,
+    tiles, count,
     X, Y, A, AT, a_parts, b_parts, a_all, b_all, own_a, own_b,
     peak_r, sum_r, peak_x, sum_x, s_pot, t_pot, row_tot, col_tot,
     half_out, half_in, row_out, row_in, row_out16, row_in16,
-    col_out, col_in, col_out16, col_in16, fin_out, fin_in,
+    spread, pair_out, pair_in, col_out, col_in, col_out16, col_in16, fin_out, fin_in,
     z_up, z_dn, z_send, xa, xb, x_send, sib_recv, mass_recv, mass_send, local,
-    half_recv, half_send, row_recv, row_send, col_recv, col_send,
+    half_recv, half_send, row_recv, row_send, col_recv, col_send, pair_sem,
 ):
     i = lax.axis_index("src")
     k = lax.axis_index("tgt")
@@ -56,6 +64,8 @@
     sibling = k + 1 - 2 * core
     up = lax.rem(i + 1, NS)
     dn = lax.rem(i + NS - 1, NS)
+    odd = lax.rem(i, 2)
+    partner = i + 1 - 2 * odd
     px, py = k // 8, lax.rem(k // 2, 4)
     pa = px * (1 - core) + py * core
     pb = py * (1 - core) + px * core
@@ -70,8 +80,10 @@
         pl.semaphore_signal(barrier, inc=1, device_id=dev, device_id_type=MESH)
     own_x = pltpu.make_async_copy(xp, X.at[pl.ds(2 * k, 2)], local.at[0])
     own_y = pltpu.make_async_copy(yp, Y.at[pl.ds(2 * i, 2)], local.at[1])
-    own_x.start()
-    own_y.start()
+    own_tiles = pltpu.make_async_copy(tiles_hbm, tiles, local.at[2])
+    own_count = pltpu.make_async_copy(count_hbm, count, local.at[3])
+    for copy in (own_y, own_x, own_tiles, own_count):
+        copy.start()
     own_x.wait()
     own_y.wait()
     pl.semaphore_wait(barrier, len(near))
@@ -84,14 +96,21 @@
     def drain(like, sem):
         pltpu.make_async_copy(like, like, sem).wait()
 
-    def z_copy(shard, q, step, direction):
-        block = Y.at[2 * shard + q // 2, pl.ds((q % 2) * 64, 64)]
-        if direction == 0:
-            return remote(block, block, z_send.at[0], z_up.at[step * 4 + q], (up, k))
-        return remote(block, block, z_send.at[1], z_dn.at[step * 4 + q], (dn, k))
-
-    def z_wait(shard, q, step, direction):
-        drain(Y.at[2 * shard + q // 2, pl.ds((q % 2) * 64, 64)], (z_up, z_dn)[direction].at[step * 4 + q])
+    def to_plane(src, dst, ssem, rsem):
+        for dx, dy, dc in PLANE:
+            to = lax.rem(px + dx, 4) * 8 + lax.rem(py + dy, 4) * 2 + lax.rem(core + dc, 2)
+            remote(src, dst, ssem, rsem, (i, to)).start()
+
+    def z_piece(shard, q):
+        return Y.at[2 * shard + q // (PIECES // 2), pl.ds((q % (PIECES // 2)) * PIECE, PIECE)]
+
+    def z_copy(shard, q, distance, direction, to):
+        block = z_piece(shard, q)
+        sem = (z_up, z_dn)[direction].at[(distance - 1) * PIECES + q]
+        return remote(block, block, z_send.at[direction], sem, (to, k))
+
+    def z_wait(shard, q, distance, direction):
+        drain(z_piece(shard, q), (z_up, z_dn)[direction].at[(distance - 1) * PIECES + q])
 
     def x_block(da, db):
         return X.at[pl.ds(2 * at(da, db), 2)]
@@ -136,26 +155,39 @@
         if step == 6:
             drain(X.at[pl.ds(0, 2 * NS)], sib_recv.at[0])
 
-    def shard_costs(n, carry):
-        shard = lax.rem(i + n, NS)
-        for half in range(2):
-            c = 2 * shard + half
-            y = Y[c]
-            for h in range(2):
-                r = c + COL_TILES * h
-                costs = scaled_cost(y, X[r])
-                AT[r] = costs
-                peak, total = peak_and_sum(costs)
-                peak_r[pl.ds(r, 1), :] = peak
-                sum_r[pl.ds(r, 1), :] = total
-        return carry
-
-    for q in range(4):
-        for direction in range(2):
-            z_copy(i, q, 0, direction).start()
+    def fixed_first(c):
+        pair = jnp.concatenate([X[c], X[c + COL_TILES]], axis=0)
+        costs = scaled_cost(Y[c], pair)
+        peak, total = peak_and_sum(costs)
+        for h in range(2):
+            r = c + COL_TILES * h
+            AT[r] = costs[:, TILE * h : TILE * (h + 1)]
+            peak_r[pl.ds(r, 1), :] = peak[:, TILE * h : TILE * (h + 1)]
+            sum_r[pl.ds(r, 1), :] = total[:, TILE * h : TILE * (h + 1)]
+
+    def fixed_second(c):
+        for h in range(2):
+            r = c + COL_TILES * h
+            A[r] = scaled_cost(X[r], Y[c])
+
+    def shards_from(low, high, *bodies):
+        def shard(n, carry):
+            for half in range(2):
+                for body in bodies:
+                    body(2 * lax.rem(i + n, NS) + half)
+            return carry
+
+        lax.fori_loop(NS + low, NS + high, shard, 0)
+
+    for q in range(PIECES):
+        for direction, to in ((0, up), (1, dn)):
+            z_copy(i, q, 1, direction, to).start()
     x_copy(x_block(0, 0), xa.at[0], 1, 0)
     x_copy(x_block(0, 0), xa.at[1], -1, 0)
     x_both(0)
+    own_tiles.wait()
+    own_count.wait()
+    spread[...] = jnp.zeros((TILE, TILE), jnp.float32)
     own_a[0:1, :] = am[:, 0:TILE].astype(jnp.float32) * LOG2E
     own_a[1:2, :] = am[:, TILE:].astype(jnp.float32) * LOG2E
     own_b[0:1, :] = bm[:, 0:TILE].astype(jnp.float32) * LOG2E
@@ -163,23 +195,22 @@
     a_parts[k] = own_a[...]
     b_parts[i] = own_b[...]
     for step in range(1, 8):
-        lo = lax.rem(i + NS - step, NS)
-        hi = lax.rem(i + step, NS)
-        for q in range(4):
-            for direction, shard in ((0, lo), (1, hi)):
-                z_wait(shard, q, step - 1, direction)
-                if step < 7 or q // 2 == direction:
-                    z_copy(shard, q, step, direction).start()
+        for q in range(PIECES):
+            for direction, shard, to in ((0, lax.rem(i + NS - step, NS), up), (1, lax.rem(i + step, NS), dn)):
+                z_wait(shard, q, step, direction)
+                if step < 7 or q // (PIECES // 2) == direction:
+                    z_copy(shard, q, step + 1, direction, to).start()
         x_step(step)
         if step == 6:
-            lax.fori_loop(NS - 3, NS + 4, shard_costs, 0)
+            to_plane(own_a, a_parts.at[k], mass_send.at[0], mass_recv.at[0])
+            shards_from(-2, 3, fixed_first, fixed_second)
         if step == 7:
-            lax.fori_loop(NS - 6, NS - 3, shard_costs, 0)
-            lax.fori_loop(4, 7, shard_costs, 0)
+            shards_from(-6, -2, fixed_first)
+            shards_from(3, 7, fixed_first)
     far = lax.rem(i + 8, NS)
-    for q in range(4):
-        z_wait(far, q, 7, q // 2)
-    lax.fori_loop(7, 10, shard_costs, 0)
+    for q in range(PIECES):
+        z_wait(far, q, 8, q // (PIECES // 2))
+    shards_from(7, 10, fixed_first)
     live_count = count[0, 0]
 
     def alive(s):
@@ -211,41 +242,39 @@
     def extra_second(s):
         A[FIXED + s] = scaled_cost(X[row_of(s)], Y[col_of(s)])
 
-    def fixed_second(c):
-        for h in range(2):
-            r = c + COL_TILES * h
-            A[r] = scaled_cost(X[r], Y[c])
-
-    def fold(first, which):
-        peak = peak_r[pl.ds(first, HALF), :]
-        owner = lax.broadcasted_iota(jnp.int32, (HALF, TILE), 0) + first
+    def fold(first, size, which):
+        peak = peak_r[pl.ds(first, size), :]
+        owner = lax.broadcasted_iota(jnp.int32, (size, TILE), 0) + first
         pick_id = row_of if which == 0 else col_of
         px = peak_x[...]
         sx = sum_x[...]
         highest = peak
         for s in range(EXTRA):
             highest = jnp.maximum(highest, jnp.where(owner == pick_id(s), px[s : s + 1], LOWEST))
-        total = sum_r[pl.ds(first, HALF), :] * jnp.exp2(peak - highest)
+        total = sum_r[pl.ds(first, size), :] * jnp.exp2(peak - highest)
         for s in range(EXTRA):
             shortfall = jnp.minimum(px[s : s + 1] - highest, 0.0)
             total = total + jnp.where(owner == pick_id(s), sx[s : s + 1] * jnp.exp2(shortfall), 0.0)
         return highest + jnp.log2(total)
 
-    def columns_of(pot):
-        rows = pot.shape[0]
-        full = jnp.concatenate([pot, jnp.zeros((TILE - rows, TILE), jnp.float32)], axis=0)
-        return full.T
-
-    def pick(cols, n):
-        lane = lax.broadcasted_iota(jnp.int32, (TILE, TILE), 1)
-        return jnp.sum(jnp.where(lane == n, cols, 0.0), axis=1, keepdims=True)
-
-    def row_extras(cols):
-        grouped(lambda s: keep_extra(s, *peak_and_sum(AT[FIXED + s] + pick(cols, col_of(s)))), EXTRA, 4)
+    def columns_of(pot, first, which):
+        spread[0:first, :] = pot[...]
+        for s in range(EXTRA):
+            spread[first + s : first + s + 1, :] = pot[pl.ds(row_of(s) if which == 0 else col_of(s), 1), :]
+        return spread[...].T
+
+    def lanes_from(cols, first):
+        return pltpu.roll(cols, lax.rem(TILE - first, TILE), 1)
+
+    def extras(cols, costs, first):
+        for g in range(EXTRA // 8):
+            for u in range(8):
+                s = 8 * g + u
+                keep_extra(s, *peak_and_sum(costs[FIXED + s] + cols[:, first + s : first + s + 1]))
 
     def row_half(cols, first):
         def group(g, carry):
-            near = pltpu.roll(cols, lax.rem(TILE - 8 * g, TILE), 1)
+            near = lanes_from(cols, 8 * g)
             for u in range(8):
                 r = 8 * g + u + first
                 peak, total = peak_and_sum(AT[r] + near[:, u : u + 1])
@@ -255,29 +284,20 @@
 
         lax.fori_loop(0, HALF // 8, group, 0)
 
-    def col_pass():
-        cols = columns_of(s_pot[...])
-
+    def col_half(cols, first):
         def group(g, carry):
-            near = pltpu.roll(cols, lax.rem(TILE - 8 * g, TILE), 1)
+            near = lanes_from(cols, 8 * g + first)
             for u in range(8):
-                c = 8 * g + u
-                first = A[c] + near[:, u : u + 1]
-                second = A[c + COL_TILES] + near[:, COL_TILES + u : COL_TILES + u + 1]
-                peak, total = peak_and_sum(jnp.concatenate([first, second], axis=0))
+                c = 8 * g + u + first
+                one = A[c] + near[:, u : u + 1]
+                two = A[c + COL_TILES] + near[:, COL_TILES + u : COL_TILES + u + 1]
+                peak = jnp.max(jnp.maximum(one, two), axis=0, keepdims=True)
+                total = jnp.sum(jnp.exp2(one - peak) + jnp.exp2(two - peak), axis=0, keepdims=True)
                 peak_r[pl.ds(c, 1), :] = peak
                 sum_r[pl.ds(c, 1), :] = total
             return carry
 
-        lax.fori_loop(0, COL_TILES // 8, group, 0)
-        grouped(lambda s: keep_extra(s, *peak_and_sum(A[FIXED + s] + pick(cols, row_of(s)))), EXTRA, 4)
-
-    def to_plane(src, dst, ssem, rsem):
-        def send(d, c):
-            remote(src, dst, ssem, rsem, (i, lax.rem(k + d, NT))).start()
-            return c
-
-        lax.fori_loop(1, NT, send, 0)
+        lax.fori_loop(0, COL_TILES // 16, group, 0)
 
     def to_line(src, dst, ssem, rsem):
         def send(d, c):
@@ -289,17 +309,19 @@
 
     mine = pl.multiple_of(HALF * core, HALF)
     other = HALF - mine
+    mine_z = pl.multiple_of(QUARTER * odd, QUARTER)
+    other_z = QUARTER - mine_z
     grouped(extra_first, EXTRA, 4)
     for it in range(ITERS):
         if it > 0:
-            cols = columns_of(t_pot[...])
-            row_extras(cols)
+            cols = columns_of(t_pot, COL_TILES, 1)
+            extras(cols, AT, COL_TILES)
             row_half(cols, other)
-        half_out[it] = fold(other, 0)
+        half_out[it] = fold(other, HALF, 0)
         remote(half_out.at[it], half_in.at[it], half_send.at[it], half_recv.at[it], (i, sibling)).start()
         if it > 0:
             row_half(cols, mine)
-        one = fold(mine, 0)
+        one = fold(mine, HALF, 0)
         drain(half_in.at[it], half_recv.at[it])
         two = half_in[it]
         top = jnp.maximum(one, two)
@@ -309,9 +331,8 @@
             row_in[k] = both
             to_plane(row_out, row_in.at[k], row_send.at[0], row_recv.at[0])
             to_line(own_b, b_parts.at[i], mass_send.at[1], mass_recv.at[1])
-            to_plane(own_a, a_parts.at[k], mass_send.at[0], mass_recv.at[0])
             grouped(extra_second, EXTRA, 4)
-            grouped(fixed_second, COL_TILES, 4)
+            shards_from(3, 14, fixed_second)
             drain(row_in.at[pl.ds(0, NT - 1)], row_recv.at[0])
             total = lse_leading(row_in[...].reshape(NS, ROW_TILES, TILE))
             drain(a_parts.at[pl.ds(0, NT - 1)], mass_recv.at[0])
@@ -328,18 +349,31 @@
         row_tot[...] = total
         s_pot[...] = a_all[...] - total
 
-        col_pass()
-        logs = fold(0, 1)
+        cols = columns_of(s_pot, ROW_TILES, 0)
+        extras(cols, A, ROW_TILES)
         if it == 0:
-            col_out[...] = logs
-            col_in[i] = logs
-            to_line(col_out, col_in.at[i], col_send.at[0], col_recv.at[0])
+            col_half(cols, other_z)
+            pair_out[...] = fold(other_z, QUARTER, 1)
+            remote(pair_out, pair_in, pair_sem.at[0], pair_sem.at[1], (partner, k)).start()
+            col_half(cols, mine_z)
+            one = fold(mine_z, QUARTER, 1)
             drain(b_parts.at[pl.ds(0, NS - 1)], mass_recv.at[1])
             for n in range(NS):
                 b_all[2 * n : 2 * n + 2, :] = b_parts[n]
+            drain(pair_in, pair_sem.at[1])
+            two = pair_in[...]
+            top = jnp.maximum(one, two)
+            both = top + jnp.log2(jnp.exp2(one - top) + jnp.exp2(two - top))
+            col_out[...] = both
+            col_in[i] = both
+            to_line(col_out, col_in.at[i], col_send.at[0], col_recv.at[0])
             drain(col_in.at[pl.ds(0, NS - 1)], col_recv.at[0])
-            total = lse_leading(col_in[...])
-        elif it + 1 < ITERS:
+            total = lse_leading(col_in[...].reshape(NS // 2, COL_TILES, TILE))
+        else:
+            col_half(cols, 0)
+            col_half(cols, QUARTER)
+            logs = fold(0, COL_TILES, 1)
+        if 0 < it < ITERS - 1:
             rest = (logs - col_tot[...]).astype(jnp.bfloat16)
             col_out16[...] = rest
             col_in16[i] = rest
@@ -359,7 +393,7 @@
         return c
 
     lax.fori_loop(0, NS - 1, send_fin, 0)
-    s_out[...] = s_pot[pl.ds(2 * k, 2), :] * LN2
+    pots[0] = s_pot[pl.ds(2 * k, 2), :] * LN2
     drain(Y.at[pl.ds(0, 15)], z_send.at[0])
     drain(Y.at[pl.ds(0, 15)], z_send.at[1])
     drain(X.at[pl.ds(0, 30)], x_send.at[0])
@@ -371,28 +405,27 @@
     drain(row_in.at[pl.ds(0, NT - 1)], row_send.at[0])
     for it in range(1, ITERS):
         drain(row_in16.at[it - 1, pl.ds(0, NT - 1)], row_send.at[it])
+    drain(pair_in, pair_sem.at[0])
     drain(col_in.at[pl.ds(0, NS - 1)], col_send.at[0])
     drain(col_in16.at[pl.ds(0, NS - 1)], col_send.at[1])
     drain(fin_in.at[pl.ds(0, NS - 1)], col_send.at[2])
     drain(fin_in.at[pl.ds(0, NS - 1)], col_recv.at[2])
-    t_out[...] = (own_b[...] - lse_leading(fin_in[...])) * LN2
+    pots[1] = (own_b[...] - lse_leading(fin_in[...])) * LN2
 
 
 def shards(src_points, src_logmass, tgt_points, tgt_logmass, tile_list, tile_count):
     f32, bf16 = jnp.float32, jnp.bfloat16
     vmem = pl.BlockSpec(memory_space=pltpu.VMEM)
-    smem = pl.BlockSpec(memory_space=pltpu.SMEM)
     hbm = pl.BlockSpec(memory_space=pltpu.HBM)
     dma = pltpu.SemaphoreType.DMA
-    s, t = pl.pallas_call(
+    pots = pl.pallas_call(
         kernel,
-        out_shape=(
-            jax.ShapeDtypeStruct((2, TILE), f32),
-            jax.ShapeDtypeStruct((2, TILE), f32),
-        ),
-        in_specs=[hbm, vmem, hbm, vmem, smem, smem],
-        out_specs=(vmem, vmem),
+        out_shape=jax.ShapeDtypeStruct((2, 2, TILE), f32),
+        in_specs=[hbm, vmem, hbm, vmem, hbm, hbm],
+        out_specs=vmem,
         scratch_shapes=[
+            pltpu.SMEM((2, SLOTS), jnp.int32),
+            pltpu.SMEM((1, 1), jnp.int32),
             pltpu.VMEM((ROW_TILES, TILE, D), bf16),
             pltpu.VMEM((COL_TILES, TILE, D), bf16),
             pltpu.VMEM((SLOTS, TILE, TILE), f32),
@@ -417,14 +450,17 @@
             pltpu.VMEM((NT, HALF, TILE), f32),
             pltpu.VMEM((ITERS - 1, HALF, TILE), bf16),
             pltpu.VMEM((ITERS - 1, NT, HALF, TILE), bf16),
-            pltpu.VMEM((COL_TILES, TILE), f32),
-            pltpu.VMEM((NS, COL_TILES, TILE), f32),
+            pltpu.VMEM((TILE, TILE), f32),
+            pltpu.VMEM((QUARTER, TILE), f32),
+            pltpu.VMEM((QUARTER, TILE), f32),
+            pltpu.VMEM((QUARTER, TILE), f32),
+            pltpu.VMEM((NS, QUARTER, TILE), f32),
             pltpu.VMEM((COL_TILES, TILE), bf16),
             pltpu.VMEM((NS, COL_TILES, TILE), bf16),
             pltpu.VMEM((NS, 2, TILE), f32),
             pltpu.VMEM((NS, 2, TILE), f32),
-            dma((32,)),
-            dma((32,)),
+            dma((8 * PIECES,)),
+            dma((8 * PIECES,)),
             dma((2,)),
             dma((4,)),
             dma((16,)),
@@ -432,13 +468,14 @@
             dma((1,)),
             dma((2,)),
             dma((2,)),
-            dma((2,)),
+            dma((4,)),
             dma((ITERS,)),
             dma((ITERS,)),
             dma((ITERS,)),
             dma((ITERS,)),
             dma((ITERS,)),
             dma((ITERS,)),
+            dma((2,)),
         ],
         compiler_params=pltpu.CompilerParams(
             collective_id=0, has_side_effects=True, vmem_limit_bytes=60 * 2**20
@@ -451,7 +488,7 @@
         tile_list.reshape(SLOTS, 2).T,
         tile_count,
     )
-    return s.reshape(1, 2 * TILE), t.reshape(1, 2 * TILE)
+    return pots[0].reshape(1, 2 * TILE), pots[1].reshape(1, 2 * TILE)
 
 
 def solution(mesh):

time: 122 us -> 112 us (0.918)
  Pallas kernels: 118 us -> 109 us
    pallas_call x1, Pallas kernels: 118 us -> 109 us  [shards(): pl.pallas_call(kernel, out_shape=jax.ShapeDtypeStruct((2, 2, TILE), f32),...]
    unnamed x6 -> x0, local copies, waits for them, and re-layouts: 1.85 us -> none
    slice x0 -> x1, local copies, waits for them, and re-layouts: none -> 1.24 us  [shards(): return (pots[0].reshape(1, 2 * TILE), pots[1].reshape(1, 2 * TILE))]
where the time goes in v3:
time: 112 us
  Pallas kernels  109 us (97%)
  between operations  1.29 us (1%)
  local copies, waits for them, and re-layouts  1.24 us (1%)
    pallas_call x1, Pallas kernels, shards(): pl.pallas_call(kernel, out_shape=jax.ShapeDtypeStruct((2, 2, TILE), f32),...  109 us

profile of v3, /device:TPU:1, one launch (start us, length us, event | category | flops | bytes accessed | tf_op | source)
XLA Modules:
  0.0 111.7 jit_solution(5901854861710027767)
XLA Ops:
  1.3 109.2 %shard_map.77 = f32[2,2,128]{2,1,0:T(2,128)} custom-call(bf16[2,128,256]{2,1,0:T(8,128)(2,1)} %bitcast.7, bf16[1,256]{1,0:T(2,128)(2,1)} %am.1, bf16[2,128,256]{2,1,0:T(8,128)(2,1)} %bitcast.8, bf16[1,256]{1,0:T(2,128)(2,1)} %bm.1, s32[2,80]{1,0:T(2,128)} %bitcast.9, s32[1,1]{1,0:T(1,128)S(6)} %copy.8.count_hbm), custom_call_target="tpu_custom_call" | custom-call | tf_op jit(solution)/shard_map/pallas_call | solution.py:421
  110.4 1.2 %fusion = (f32[1,2,128]{2,1,0:T(2,128)}, f32[1,2,128]{2,1,0:T(2,128)}) fusion(f32[2,2,128]{2,1,0:T(2,128)} %shard_map.77), kind=kLoop, calls=%fused_computation | loop fusion | bytes 4096 | tf_op jit(solution)/shard_map/slice | solution.py:491

commit v4 on v3

--- a/solution.py
+++ b/solution.py
@@ -264,7 +264,7 @@
         return spread[...].T
 
     def lanes_from(cols, first):
-        return pltpu.roll(cols, lax.rem(TILE - first, TILE), 1)
+        return cols if isinstance(first, int) else pltpu.roll(cols, lax.rem(TILE - first, TILE), 1)
 
     def extras(cols, costs, first):
         for g in range(EXTRA // 8):
@@ -273,31 +273,21 @@
                 keep_extra(s, *peak_and_sum(costs[FIXED + s] + cols[:, first + s : first + s + 1]))
 
     def row_half(cols, first):
-        def group(g, carry):
-            near = lanes_from(cols, 8 * g)
-            for u in range(8):
-                r = 8 * g + u + first
-                peak, total = peak_and_sum(AT[r] + near[:, u : u + 1])
-                peak_r[pl.ds(r, 1), :] = peak
-                sum_r[pl.ds(r, 1), :] = total
-            return carry
-
-        lax.fori_loop(0, HALF // 8, group, 0)
-
-    def col_half(cols, first):
-        def group(g, carry):
-            near = lanes_from(cols, 8 * g + first)
-            for u in range(8):
-                c = 8 * g + u + first
-                one = A[c] + near[:, u : u + 1]
-                two = A[c + COL_TILES] + near[:, COL_TILES + u : COL_TILES + u + 1]
-                peak = jnp.max(jnp.maximum(one, two), axis=0, keepdims=True)
-                total = jnp.sum(jnp.exp2(one - peak) + jnp.exp2(two - peak), axis=0, keepdims=True)
-                peak_r[pl.ds(c, 1), :] = peak
-                sum_r[pl.ds(c, 1), :] = total
-            return carry
-
-        lax.fori_loop(0, COL_TILES // 16, group, 0)
+        for c in range(HALF):
+            peak, total = peak_and_sum(AT[c + first] + cols[:, c : c + 1])
+            peak_r[pl.ds(c + first, 1), :] = peak
+            sum_r[pl.ds(c + first, 1), :] = total
+
+    def col_range(cols, first, size):
+        near = lanes_from(cols, first)
+        for u in range(size):
+            c = u + first
+            one = A[c] + near[:, u : u + 1]
+            two = A[c + COL_TILES] + near[:, COL_TILES + u : COL_TILES + u + 1]
+            peak = jnp.max(jnp.maximum(one, two), axis=0, keepdims=True)
+            total = jnp.sum(jnp.exp2(one - peak) + jnp.exp2(two - peak), axis=0, keepdims=True)
+            peak_r[pl.ds(c, 1), :] = peak
+            sum_r[pl.ds(c, 1), :] = total
 
     def to_line(src, dst, ssem, rsem):
         def send(d, c):
@@ -311,7 +301,7 @@
     other = HALF - mine
     mine_z = pl.multiple_of(QUARTER * odd, QUARTER)
     other_z = QUARTER - mine_z
-    grouped(extra_first, EXTRA, 4)
+    grouped(extra_first, EXTRA, 8)
     for it in range(ITERS):
         if it > 0:
             cols = columns_of(t_pot, COL_TILES, 1)
@@ -352,10 +342,10 @@
         cols = columns_of(s_pot, ROW_TILES, 0)
         extras(cols, A, ROW_TILES)
         if it == 0:
-            col_half(cols, other_z)
+            col_range(cols, other_z, QUARTER)
             pair_out[...] = fold(other_z, QUARTER, 1)
             remote(pair_out, pair_in, pair_sem.at[0], pair_sem.at[1], (partner, k)).start()
-            col_half(cols, mine_z)
+            col_range(cols, mine_z, QUARTER)
             one = fold(mine_z, QUARTER, 1)
             drain(b_parts.at[pl.ds(0, NS - 1)], mass_recv.at[1])
             for n in range(NS):
@@ -370,8 +360,7 @@
             drain(col_in.at[pl.ds(0, NS - 1)], col_recv.at[0])
             total = lse_leading(col_in[...].reshape(NS // 2, COL_TILES, TILE))
         else:
-            col_half(cols, 0)
-            col_half(cols, QUARTER)
+            col_range(cols, 0, COL_TILES)
             logs = fold(0, COL_TILES, 1)
         if 0 < it < ITERS - 1:
             rest = (logs - col_tot[...]).astype(jnp.bfloat16)

time: 112 us -> 108 us (0.964)
  Pallas kernels: 109 us -> 105 us
    pallas_call x1, Pallas kernels: 109 us -> 105 us  [shards(): pl.pallas_call(kernel, out_shape=jax.ShapeDtypeStruct((2, 2, TILE), f32),...]
where the time goes in v4:
time: 108 us
  Pallas kernels  105 us (97%)
  between operations  1.29 us (1%)
  local copies, waits for them, and re-layouts  1.24 us (1%)
    pallas_call x1, Pallas kernels, shards(): pl.pallas_call(kernel, out_shape=jax.ShapeDtypeStruct((2, 2, TILE), f32),...  105 us

profile of v4, /device:TPU:1, one launch (start us, length us, event | category | flops | bytes accessed | tf_op | source)
XLA Modules:
  0.0 107.7 jit_solution(11793191330034855398)
XLA Ops:
  1.3 105.2 %shard_map.77 = f32[2,2,128]{2,1,0:T(2,128)} custom-call(bf16[2,128,256]{2,1,0:T(8,128)(2,1)} %bitcast.7, bf16[1,256]{1,0:T(2,128)(2,1)} %am.1, bf16[2,128,256]{2,1,0:T(8,128)(2,1)} %bitcast.8, bf16[1,256]{1,0:T(2,128)(2,1)} %bm.1, s32[2,80]{1,0:T(2,128)} %bitcast.9, s32[1,1]{1,0:T(1,128)S(6)} %copy.8.count_hbm), custom_call_target="tpu_custom_call" | custom-call | tf_op jit(solution)/shard_map/pallas_call | solution.py:410
  106.5 1.2 %fusion = (f32[1,2,128]{2,1,0:T(2,128)}, f32[1,2,128]{2,1,0:T(2,128)}) fusion(f32[2,2,128]{2,1,0:T(2,128)} %shard_map.77), kind=kLoop, calls=%fused_computation | loop fusion | bytes 4096 | tf_op jit(solution)/shard_map/slice | solution.py:480

commit v5 on v4

--- a/solution.py
+++ b/solution.py
@@ -84,7 +84,6 @@
     own_count = pltpu.make_async_copy(count_hbm, count, local.at[3])
     for copy in (own_y, own_x, own_tiles, own_count):
         copy.start()
-    own_x.wait()
     own_y.wait()
     pl.semaphore_wait(barrier, len(near))
 
@@ -182,6 +181,7 @@
     for q in range(PIECES):
         for direction, to in ((0, up), (1, dn)):
             z_copy(i, q, 1, direction, to).start()
+    own_x.wait()
     x_copy(x_block(0, 0), xa.at[0], 1, 0)
     x_copy(x_block(0, 0), xa.at[1], -1, 0)
     x_both(0)
@@ -210,7 +210,9 @@
     far = lax.rem(i + 8, NS)
     for q in range(PIECES):
         z_wait(far, q, 8, q // (PIECES // 2))
-    shards_from(7, 10, fixed_first)
+    for n in range(7, 10):
+        for half in range(2):
+            fixed_first(2 * lax.rem(i + n, NS) + half)
     live_count = count[0, 0]
 
     def alive(s):
@@ -301,7 +303,7 @@
     other = HALF - mine
     mine_z = pl.multiple_of(QUARTER * odd, QUARTER)
     other_z = QUARTER - mine_z
-    grouped(extra_first, EXTRA, 8)
+    grouped(extra_first, EXTRA, 16)
     for it in range(ITERS):
         if it > 0:
             cols = columns_of(t_pot, COL_TILES, 1)
@@ -323,11 +325,11 @@
             to_line(own_b, b_parts.at[i], mass_send.at[1], mass_recv.at[1])
             grouped(extra_second, EXTRA, 4)
             shards_from(3, 14, fixed_second)
-            drain(row_in.at[pl.ds(0, NT - 1)], row_recv.at[0])
-            total = lse_leading(row_in[...].reshape(NS, ROW_TILES, TILE))
             drain(a_parts.at[pl.ds(0, NT - 1)], mass_recv.at[0])
             for n in range(NT):
                 a_all[2 * n : 2 * n + 2, :] = a_parts[n]
+            drain(row_in.at[pl.ds(0, NT - 1)], row_recv.at[0])
+            total = lse_leading(row_in[...].reshape(NS, ROW_TILES, TILE))
         else:
             rest = (both - row_tot[pl.ds(mine, HALF), :]).astype(jnp.bfloat16)
             row_out16[it - 1] = rest

time: 108 us -> 107 us (level)
  no operation moved by 1% of the time
where the time goes in v5:
time: 107 us
  Pallas kernels  105 us (98%)
  between operations  1.29 us (1%)
  local copies, waits for them, and re-layouts  1.24 us (1%)
    pallas_call x1, Pallas kernels, shards(): pl.pallas_call(kernel, out_shape=jax.ShapeDtypeStruct((2, 2, TILE), f32),...  105 us

profile of v5, /device:TPU:1, one launch (start us, length us, event | category | flops | bytes accessed | tf_op | source)
XLA Modules:
  0.0 107.2 jit_solution(15439427989241971370)
XLA Ops:
  1.3 104.7 %shard_map.77 = f32[2,2,128]{2,1,0:T(2,128)} custom-call(bf16[2,128,256]{2,1,0:T(8,128)(2,1)} %bitcast.7, bf16[1,256]{1,0:T(2,128)(2,1)} %am.1, bf16[2,128,256]{2,1,0:T(8,128)(2,1)} %bitcast.8, bf16[1,256]{1,0:T(2,128)(2,1)} %bm.1, s32[2,80]{1,0:T(2,128)} %bitcast.9, s32[1,1]{1,0:T(1,128)S(6)} %copy.8.count_hbm), custom_call_target="tpu_custom_call" | custom-call | tf_op jit(solution)/shard_map/pallas_call | solution.py:412
  105.9 1.2 %fusion = (f32[1,2,128]{2,1,0:T(2,128)}, f32[1,2,128]{2,1,0:T(2,128)}) fusion(f32[2,2,128]{2,1,0:T(2,128)} %shard_map.77), kind=kLoop, calls=%fused_computation | loop fusion | bytes 4096 | tf_op jit(solution)/shard_map/slice | solution.py:482
